TPU v7x, 32 devices: a whole 2x2x4 slice. The times are simulated.
32 devices in a mesh: rep: 2 (over x), gx: 16 (over z, y, core).
Axes of the slice: x: 2, y: 2, z: 4, core: 2. Of those that a mesh axis runs over, the one named last changes fastest.
Arguments:
- inputs: bfloat16 [2, 64, 18432], P(None, 'rep', 'gx'), parts along dimension 1, may hold values from -450 to 450, as said below
- gain: bfloat16 [18432], P('gx'), may hold values from 0.5 to 1.5
- w_query: bfloat16 [18432, 12288], P(None, 'gx'), may hold values from -0.046875 to 0.046875
- w_keyval: bfloat16 [18432, 512], P('gx'), may hold values from -0.046875 to 0.046875
- w_out: bfloat16 [12288, 18432], P(None, 'gx'), may hold values from -0.0546875 to 0.0546875
- key_cache: bfloat16 [64, 2048, 256], P(('rep', 'gx')), parts along dimension 0, may hold values from -240 to 240
- value_cache: bfloat16 [64, 2048, 256], P(('rep', 'gx')), parts along dimension 0, may hold values from -6 to 6
- lengths: int32 [64], P(('rep', 'gx')), parts along dimension 0, may hold values from 1 to 2048, 32768 in all
Outputs:
- branch: bfloat16 [2, 64, 18432], P(None, 'rep', 'gx'), parts along dimension 1
There are 2 independent parts, one for each index of `rep`. A program takes and returns all parts, laid end to end along the dimension named above; an argument that names none is the same for every part. Nothing has to cross between parts.
Inputs may be any that keep to these rules, and one draw needn't show every extreme that they name: `inputs`: activations. The lengths of each part along rep sum to 32768; at least one row has exactly 2048.
All inputs are finite; a program needn't handle non-finite values. No bound on the sum of `lengths` on one device may be relied on, other than what follows from the above.
Results may differ from a plain program's by a relative error of at most 0.0065.
The roundings to bfloat16 on the way count: a program that leaves them out, or rounds other values in their place, can miss the bound.
Values may be sent and summed in bfloat16 or wider, within the bound.
A program may use at most 192 MiB of HBM per device.

v0:
```python
import jax
import jax.numpy as jnp
from jax import lax
from jax.sharding import PartitionSpec as P

D = 18432
H = 48
DH = 256


EPS = 1e-05


def collect_keyval(local_normed, w_keyval):
    summed = lax.psum_scatter(
        jnp.einsum("srk,kc->rsc", local_normed, w_keyval, preferred_element_type=jnp.float32),
        "gx",
        scatter_dimension=0,
        tiled=True,
    )
    return jnp.transpose(summed, (1, 0, 2)).astype(jnp.bfloat16)


def project(block, gain, w_query, w_keyval):
    widened = block.astype(jnp.float32)
    totals, squares = lax.psum((jnp.sum(widened, -1), jnp.sum(widened * widened, -1)), "gx")
    row_mean = (totals / D)[..., None]
    row_square = (squares / D)[..., None]
    normed = (
        (widened - row_mean)
        * lax.rsqrt(row_square - row_mean * row_mean + EPS)
        * gain.astype(jnp.float32)
    ).astype(jnp.bfloat16)
    query_zero = jnp.zeros((block.shape[0], block.shape[1], w_query.shape[1]), jnp.float32)
    portion = lax.all_gather(normed, "gx", axis=2, tiled=True)
    extent = portion.shape[2]
    flat = portion.reshape(-1, extent)
    query_part = jnp.dot(flat, w_query, preferred_element_type=jnp.float32).reshape(
        query_zero.shape
    )
    keyvals = collect_keyval(normed, w_keyval)
    return (query_part.astype(jnp.bfloat16), keyvals)


def route(queries):
    return lax.all_to_all(queries, "gx", split_axis=1, concat_axis=2, tiled=True)


def attend(queries, key_cache, value_cache, lengths, fresh_keys, fresh_values, first_step):
    steps_here = queries.shape[0]
    rows_here = queries.shape[1]
    recent_count = fresh_keys.shape[0]
    scale = DH ** (-0.5)
    grid = queries.reshape(steps_here, rows_here, H, DH)
    cached = (
        jnp.einsum("srhd,rcd->srhc", grid, key_cache, preferred_element_type=jnp.float32) * scale
    )
    valid = (
        lax.broadcasted_iota(jnp.int32, (1, rows_here, 1, key_cache.shape[1]), 3)
        < lengths[None, :, None, None]
    )
    cached = jnp.where(valid, cached, -jnp.inf)
    recent = (
        jnp.einsum("srhd,trd->srht", grid, fresh_keys, preferred_element_type=jnp.float32) * scale
    )
    allowed = (
        lax.broadcasted_iota(jnp.int32, (steps_here, 1, 1, recent_count), 3)
        <= lax.broadcasted_iota(jnp.int32, (steps_here, 1, 1, recent_count), 0) + first_step
    )
    recent = jnp.where(allowed, recent, -jnp.inf)
    top = jnp.maximum(jnp.max(cached, -1, keepdims=True), jnp.max(recent, -1, keepdims=True))
    cached_exp = jnp.exp(cached - top)
    recent_exp = jnp.exp(recent - top)
    denom = jnp.sum(cached_exp, -1, keepdims=True) + jnp.sum(recent_exp, -1, keepdims=True)
    cached_prob = (cached_exp / denom).astype(jnp.bfloat16)
    recent_prob = (recent_exp / denom).astype(jnp.bfloat16)
    result = jnp.einsum(
        "srhc,rcd->srhd", cached_prob, value_cache, preferred_element_type=jnp.float32
    )
    result = result + jnp.einsum(
        "srht,trd->srhd", recent_prob, fresh_values, preferred_element_type=jnp.float32
    )
    return result.astype(jnp.bfloat16).reshape(steps_here, rows_here, H * DH)


def finish(attended, w_out):
    portion = lax.all_gather(attended, "gx", axis=1, tiled=True)
    flat = portion.reshape(-1, portion.shape[2])
    product = jnp.dot(flat, w_out, preferred_element_type=jnp.float32)
    return product.reshape(portion.shape[0], portion.shape[1], w_out.shape[1]).astype(jnp.bfloat16)


def body(inputs, gain, w_query, w_keyval, w_out, key_cache, value_cache, lengths):
    results = []
    key_list = []
    value_list = []
    for step_index in range(inputs.shape[0]):
        queries, keyvals = project(inputs[step_index : step_index + 1], gain, w_query, w_keyval)
        queries = route(queries)
        key_list.append(keyvals[:, :, :DH])
        value_list.append(keyvals[:, :, DH:])
        attended = attend(
            queries,
            key_cache,
            value_cache,
            lengths,
            jnp.concatenate(key_list, 0),
            jnp.concatenate(value_list, 0),
            step_index,
        )
        results.append(finish(attended, w_out))
    return jnp.concatenate(results, 0)


def solution(mesh):
    in_specs = (
        P(None, "rep", "gx"),
        P("gx"),
        P(None, "gx"),
        P("gx", None),
        P(None, "gx"),
        P(("rep", "gx"), None, None),
        P(("rep", "gx"), None, None),
        P(("rep", "gx")),
    )
    out_specs = P(None, "rep", "gx")
    return jax.shard_map(body, mesh=mesh, in_specs=in_specs, out_specs=out_specs, check_vma=False)
```

profile of v0, /device:TPU:0, one launch (start us, length us, event | category | flops | bytes accessed | tf_op | source)
XLA Modules:
  0.0 245.1 jit_solution(6279512406806527111)
XLA Ops:
  6.6 0.8 convert_element_type.100
  7.4 1.2 convert_reduce_fusion.1
  8.6 34.9 %all-reduce.3 = (f32[1,32]{1,0:T(1,128)S(1)}, f32[1,32]{1,0:T(1,128)S(1)}, f32[1,32]{1,0:T(1,128)S(1)}, f32[1,32]{1,0:T(1,128)S(1)}) all-reduce(f32[1,32]{1,0:T(1,128)S(1)} %bitcast.180, f32[1,32]{1,0:T(1,128)S(1)} %bitcast.181, f32[1,32]{1,0:T(1,128)S(1)} %bitcast.179, ...), channel_id=1, replica_groups=mesh['rep'=2,'gx'=16] {'gx'}, use_global_device_ids=true, to_apply=%region_10.11 | all-reduce | flops 128 | bytes 1024 | tf_op jit(solution)/shard_map/psum | solution.py:26
  43.5 1.7 fusion.44
  45.3 0.7 all-gather.3.cloned.1.call-update
  46.0 1.6 convolution_bitcast_fusion.2
  47.6 1.2 convolution_bitcast_fusion.3
  48.9 58.9 %all-reduce.5 = (bf16[32,1,512]{2,0,1:T(8,128)(2,1)S(1)}, bf16[32,1,512]{2,0,1:T(8,128)(2,1)S(1)}) all-reduce(f32[32,1,512]{2,0,1:T(8,128)S(1)} %convolution_bitcast_fusion.2, f32[32,1,512]{2,0,1:T(8,128)S(1)} %convolution_bitcast_fusion.3), channel_id=3, replica_groups=mesh['rep'=2,'gx'=16] {'gx'}, use_global_device_ids=true, to_apply=%region_12.13.clone | all-reduce | flops 32768 | bytes 196608
  109.1 14.4 %fusion.21 = bf16[1,32,768]{2,1,0:T(8,128)(2,1)S(1)} fusion(bf16[18432,768]{1,0:T(8,128)(2,1)} %param.10, bf16[1,32,18432]{2,1,0:T(8,128)(2,1)} %all-gather.5.cloned.1.call-done), kind=kOutput, calls=%fused_computation.26 | convolution fusion | flops 905994240 | bytes 29540352 | tf_op jit(solution)/shard_map/dot_general | solution.py:38
  124.1 0.9 reduce.14
  125.7 3.5 %all-to-all-start.1 = ((bf16[16,2,768]{2,1,0:T(2,128)(2,1)}), bf16[16,2,768]{2,1,0:T(2,128)(2,1)S(1)}, u32[]{:S(2)}, u32[]{:S(2)}) async-start(bf16[16,2,768]{2,1,0:T(2,128)(2,1)} %reshape.295), calls=%async_computation.1 | async-start | bytes 98304 | tf_op jit(solution)/shard_map/all_to_all | solution.py:46
  129.2 14.3 %fusion.24 = bf16[1,32,768]{2,1,0:T(8,128)(2,1)S(1)} fusion(bf16[18432,768]{1,0:T(8,128)(2,1)} %param.10, bf16[1,32,18432]{2,1,0:T(8,128)(2,1)} %all-gather.3.cloned.1.call-done), kind=kOutput, calls=%fused_computation.27 | convolution fusion | flops 905994240 | bytes 29540352 | tf_op jit(solution)/shard_map/dot_general | solution.py:38
  143.5 0.9 reduce.15
  144.4 0.6 reshape.297
  145.1 6.0 %all-to-all-start = ((bf16[16,2,768]{2,1,0:T(2,128)(2,1)}), bf16[16,2,768]{2,1,0:T(2,128)(2,1)S(1)}, u32[]{:S(2)}, u32[]{:S(2)}) async-start(bf16[16,2,768]{2,1,0:T(2,128)(2,1)} %reshape.297), calls=%async_computation | async-start | bytes 98304 | tf_op jit(solution)/shard_map/all_to_all | solution.py:46
  151.5 6.4 %all-to-all-done = bf16[16,2,768]{2,1,0:T(2,128)(2,1)S(1)} async-done(((bf16[16,2,768]{2,1,0:T(2,128)(2,1)}), bf16[16,2,768]{2,1,0:T(2,128)(2,1)S(1)}, u32[]{:S(2)}, u32[]{:S(2)}) %all-to-all-start) | async-done | bytes 49184 | tf_op jit(solution)/shard_map/all_to_all | solution.py:46
  158.4 0.8 fusion.78
  159.2 0.8 fusion.76
  161.5 25.8 %all_gather.15 = bf16[1,32,12288]{2,0,1:T(2,128)(2,1)S(1)} all-gather(bf16[1,2,12288]{2,0,1:T(2,128)(2,1)S(1)} %reshape.286), channel_id=1, replica_groups=mesh['rep'=2,'gx'=16] {'gx'}, dimensions={1}, use_global_device_ids=true | all-gather | bytes 835584 | tf_op jit(solution)/shard_map/all_gather | solution.py:87
  187.7 2.1 fusion.28
  189.8 24.2 %all_gather.13 = bf16[1,32,12288]{2,0,1:T(2,128)(2,1)S(1)} all-gather(bf16[1,2,12288]{2,0,1:T(2,128)(2,1)S(1)} %reshape.285), channel_id=1, replica_groups=mesh['rep'=2,'gx'=16] {'gx'}, dimensions={1}, use_global_device_ids=true | all-gather | bytes 835584 | tf_op jit(solution)/shard_map/all_gather | solution.py:87
  214.0 11.7 %fusion.7 = bf16[1,32,1152]{2,1,0:T(8,128)(2,1)S(1)} fusion(bf16[12288,1152]{1,0:T(8,128)(2,1)} %param.12, bf16[1,32,12288]{2,0,1:T(2,128)(2,1)S(1)} %all_gather.15), kind=kOutput, calls=%fused_computation.11 | convolution fusion | flops 906006528 | bytes 29171712 | tf_op jit(solution)/shard_map/dot_general | solution.py:89
  225.7 11.8 %fusion.6 = bf16[1,32,1152]{2,1,0:T(8,128)(2,1)S(1)} fusion(bf16[12288,1152]{1,0:T(8,128)(2,1)} %param.12, bf16[1,32,12288]{2,0,1:T(2,128)(2,1)S(1)} %all_gather.13), kind=kOutput, calls=%fused_computation.10 | convolution fusion | flops 906006528 | bytes 29171712 | tf_op jit(solution)/shard_map/dot_general | solution.py:89
  237.5 0.7 pad_maximum_fusion
  (59 shorter events, 4.9 us)
Async XLA Ops:
  6.5 151.8 %copy-start = (bf16[2,2048,256]{2,1,0:T(8,128)(2,1)S(1)}, bf16[2,2048,256]{2,1,0:T(8,128)(2,1)}, u32[]{:S(2)}) copy-start(bf16[2,2048,256]{2,1,0:T(8,128)(2,1)} %param.13) | copy-start | bytes 6291460
  6.5 101.2 %copy-start.5 = (u32[32]{0:T(128)S(1)}, u32[32]{0:T(128)}, u32[]{:S(2)}) copy-start(u32[32]{0:T(128)} %constant.25) | copy-start | bytes 388
  6.5 41.1 %copy-start.2 = (bf16[1152,512]{1,0:T(8,128)(2,1)S(1)}, bf16[1152,512]{1,0:T(8,128)(2,1)}, u32[]{:S(2)}) copy-start(bf16[1152,512]{1,0:T(8,128)(2,1)} %param.11) | copy-start | bytes 3538948
  6.5 42.3 %copy-start.3 = (s32[2]{0:T(128)S(1)}, s32[2]{0:T(128)}, u32[]{:S(2)}) copy-start(s32[2]{0:T(128)} %param.15) | copy-start | bytes 28
  6.5 102.5 %all-gather.5.cloned.1.call-start = ((), (), s32[]{:S(2)}) async-start(), calls=%async_computation.3 | async-start | bytes 1253376 | tf_op jit(solution)/shard_map/all_gather | solution.py:35
  45.2 83.9 %all-gather.3.cloned.1.call-start = ((), (), s32[]{:S(2)}) async-start(), calls=%async_computation.2 | async-start | bytes 1253376 | tf_op jit(solution)/shard_map/all_gather | solution.py:35
  125.7 19.4 %all-to-all-start.1 = ((bf16[16,2,768]{2,1,0:T(2,128)(2,1)}), bf16[16,2,768]{2,1,0:T(2,128)(2,1)S(1)}, u32[]{:S(2)}, u32[]{:S(2)}) async-start(bf16[16,2,768]{2,1,0:T(2,128)(2,1)} %reshape.295), calls=%async_computation.1 | async-start | bytes 98304 | tf_op jit(solution)/shard_map/all_to_all | solution.py:46
  145.1 12.7 %all-to-all-start = ((bf16[16,2,768]{2,1,0:T(2,128)(2,1)}), bf16[16,2,768]{2,1,0:T(2,128)(2,1)S(1)}, u32[]{:S(2)}, u32[]{:S(2)}) async-start(bf16[16,2,768]{2,1,0:T(2,128)(2,1)} %reshape.297), calls=%async_computation | async-start | bytes 98304 | tf_op jit(solution)/shard_map/all_to_all | solution.py:46
  159.2 1.6 copy-start.4
  225.7 12.5 %copy-start.1 = (bf16[2,2048,256]{2,1,0:T(8,128)(2,1)S(1)}, bf16[2,2048,256]{2,1,0:T(8,128)(2,1)}, u32[]{:S(2)}) copy-start(bf16[2,2048,256]{2,1,0:T(8,128)(2,1)} %param.13) | copy-start | bytes 6291460
Sparse Core Ops, SparseCore 0:
  45.4 36.1 all-gather.4
  83.7 37.1 all-gather.2
where the time goes:
time: 246 us; the launch traced here: 245 us
  blocking collectives  144 us (59%)
  matrix products  59.8 us (24%)
  between operations  14.3 us (6%)
  starting transfers between devices  9.52 us (4%)
  waiting for transfers between devices  7.12 us (3%)
  other arithmetic  6.88 us (3%)
  local copies, waits for them, and re-layouts  3.72 us (2%)
    unnamed x1, blocking collectives  58.9 us
    all_gather x2, blocking collectives, finish(): portion = lax.all_gather(attended, 'gx', axis=1, tiled=True)  50 us
    psum x1, blocking collectives, project(): lax.psum((jnp.sum(widened, -1), jnp.sum(widened * widened, -1)), 'gx')  34.9 us
    dot_general x2, matrix products, project(): jnp.dot(flat, w_query, preferred_element_type=jnp.float32)  28.7 us
    dot_general x2, matrix products, finish(): product = jnp.dot(flat, w_out, preferred_element_type=jnp.float32)  23.6 us
    all_to_all x2, starting transfers between devices, route(): lax.all_to_all(queries, 'gx', split_axis=1, concat_axis=2, tiled=True)  9.44 us
    all_to_all x2, waiting for transfers between devices, route(): lax.all_to_all(queries, 'gx', split_axis=1, concat_axis=2, tiled=True)  6.36 us
  transfers between devices with their start and end apart: 4, of which 1 were waited for; matrix products, arithmetic and copies ran while one was open for 15% of the time, Pallas kernels for 0%

commit v1 on v0

--- a/solution.py
+++ b/solution.py
@@ -1,6 +1,9 @@
 import jax
 import jax.numpy as jnp
+import numpy as np
 from jax import lax
+from jax.experimental import pallas as pl
+from jax.experimental.pallas import tpu as pltpu
 from jax.sharding import PartitionSpec as P
 
 D = 18432
@@ -31,27 +34,20 @@
         * lax.rsqrt(row_square - row_mean * row_mean + EPS)
         * gain.astype(jnp.float32)
     ).astype(jnp.bfloat16)
-    query_zero = jnp.zeros((block.shape[0], block.shape[1], w_query.shape[1]), jnp.float32)
     portion = lax.all_gather(normed, "gx", axis=2, tiled=True)
-    extent = portion.shape[2]
-    flat = portion.reshape(-1, extent)
+    flat = portion.reshape(-1, portion.shape[2])
     query_part = jnp.dot(flat, w_query, preferred_element_type=jnp.float32).reshape(
-        query_zero.shape
+        block.shape[0], block.shape[1], w_query.shape[1]
     )
     keyvals = collect_keyval(normed, w_keyval)
     return (query_part.astype(jnp.bfloat16), keyvals)
 
 
-def route(queries):
-    return lax.all_to_all(queries, "gx", split_axis=1, concat_axis=2, tiled=True)
-
-
-def attend(queries, key_cache, value_cache, lengths, fresh_keys, fresh_values, first_step):
-    steps_here = queries.shape[0]
+def attend(queries, key_cache, value_cache, lengths, fresh_keys, fresh_values):
+    steps = queries.shape[0]
     rows_here = queries.shape[1]
-    recent_count = fresh_keys.shape[0]
     scale = DH ** (-0.5)
-    grid = queries.reshape(steps_here, rows_here, H, DH)
+    grid = queries.reshape(steps, rows_here, H, DH)
     cached = (
         jnp.einsum("srhd,rcd->srhc", grid, key_cache, preferred_element_type=jnp.float32) * scale
     )
@@ -63,9 +59,8 @@
     recent = (
         jnp.einsum("srhd,trd->srht", grid, fresh_keys, preferred_element_type=jnp.float32) * scale
     )
-    allowed = (
-        lax.broadcasted_iota(jnp.int32, (steps_here, 1, 1, recent_count), 3)
-        <= lax.broadcasted_iota(jnp.int32, (steps_here, 1, 1, recent_count), 0) + first_step
+    allowed = lax.broadcasted_iota(jnp.int32, (steps, 1, 1, steps), 3) <= lax.broadcasted_iota(
+        jnp.int32, (steps, 1, 1, steps), 0
     )
     recent = jnp.where(allowed, recent, -jnp.inf)
     top = jnp.maximum(jnp.max(cached, -1, keepdims=True), jnp.max(recent, -1, keepdims=True))
@@ -80,7 +75,7 @@
     result = result + jnp.einsum(
         "srht,trd->srhd", recent_prob, fresh_values, preferred_element_type=jnp.float32
     )
-    return result.astype(jnp.bfloat16).reshape(steps_here, rows_here, H * DH)
+    return result.astype(jnp.bfloat16).reshape(steps, rows_here, H * DH)
 
 
 def finish(attended, w_out):
@@ -91,25 +86,12 @@
 
 
 def body(inputs, gain, w_query, w_keyval, w_out, key_cache, value_cache, lengths):
-    results = []
-    key_list = []
-    value_list = []
-    for step_index in range(inputs.shape[0]):
-        queries, keyvals = project(inputs[step_index : step_index + 1], gain, w_query, w_keyval)
-        queries = route(queries)
-        key_list.append(keyvals[:, :, :DH])
-        value_list.append(keyvals[:, :, DH:])
-        attended = attend(
-            queries,
-            key_cache,
-            value_cache,
-            lengths,
-            jnp.concatenate(key_list, 0),
-            jnp.concatenate(value_list, 0),
-            step_index,
-        )
-        results.append(finish(attended, w_out))
-    return jnp.concatenate(results, 0)
+    queries, keyvals = project(inputs, gain, w_query, w_keyval)
+    queries = lax.all_to_all(queries, "gx", split_axis=1, concat_axis=2, tiled=True)
+    attended = attend(
+        queries, key_cache, value_cache, lengths, keyvals[:, :, :DH], keyvals[:, :, DH:]
+    )
+    return finish(attended, w_out)
 
 
 def solution(mesh):

time: 246 us -> 197 us (0.80)
  blocking collectives: 144 us -> 93.9 us
  waiting for transfers between devices: 7.12 us -> 44.5 us
  matrix products: 59.8 us -> 34 us
  starting transfers between devices: 9.52 us -> 3.55 us
  other arithmetic: 6.88 us -> 4.07 us
    all_gather x2 -> x0, blocking collectives: 50 us -> none  [finish(): portion = lax.all_gather(attended, 'gx', axis=1, tiled=True)]
    all_gather x0 -> x1, waiting for transfers between devices: none -> 37.2 us  [finish(): portion = lax.all_gather(attended, 'gx', axis=1, tiled=True)]
    dot_general x2 -> x1, matrix products: 28.7 us -> 14.7 us  [project(): jnp.dot(flat, w_query, preferred_element_type=jnp.float32)]
    dot_general x2 -> x1, matrix products: 23.6 us -> 15.8 us  [finish(): product = jnp.dot(flat, w_out, preferred_element_type=jnp.float32)]
    all_to_all x2 -> x1, starting transfers between devices: 9.44 us -> 3.51 us  [body(): lax.all_to_all(queries, 'gx', split_axis=1, concat_axis=2, tiled=True)]
    all_to_all x2 -> x1, waiting for transfers between devices: 6.36 us -> 7.27 us  [body(): lax.all_to_all(queries, 'gx', split_axis=1, concat_axis=2, tiled=True)]
  transfers between devices with their start and end apart: 4 -> 3, of which waited for: 1 -> 2; matrix products, arithmetic and copies ran while one was open for 15% -> 1% of each run, Pallas kernels for 0% -> 0%
where the time goes in v1:
time: 197 us; the launch traced here: 196 us
  blocking collectives  93.9 us (48%)
  waiting for transfers between devices  44.5 us (23%)
  matrix products  34 us (17%)
  between operations  14.1 us (7%)
  other arithmetic  4.07 us (2%)
  starting transfers between devices  3.55 us (2%)
  local copies, waits for them, and re-layouts  2.18 us (1%)
    unnamed x1, blocking collectives  59 us
    all_gather x1, waiting for transfers between devices, finish(): portion = lax.all_gather(attended, 'gx', axis=1, tiled=True)  37.2 us
    psum x1, blocking collectives, project(): lax.psum((jnp.sum(widened, -1), jnp.sum(widened * widened, -1)), 'gx')  34.9 us
    dot_general x1, matrix products, finish(): product = jnp.dot(flat, w_out, preferred_element_type=jnp.float32)  15.8 us
    dot_general x1, matrix products, project(): jnp.dot(flat, w_query, preferred_element_type=jnp.float32)  14.7 us
    all_to_all x1, waiting for transfers between devices, body(): lax.all_to_all(queries, 'gx', split_axis=1, concat_axis=2, tiled=True)  7.27 us
  transfers between devices with their start and end apart: 3, of which 2 were waited for; matrix products, arithmetic and copies ran while one was open for 1% of the time, Pallas kernels for 0%

profile of v1, /device:TPU:0, one launch (start us, length us, event | category | flops | bytes accessed | tf_op | source)
XLA Modules:
  0.0 196.4 jit_solution(6578755582585536243)
XLA Ops:
  6.5 1.2 convert_reduce_fusion
  7.7 0.7 convert_element_type.31
  8.4 34.9 %all-reduce.1 = (f32[2,32]{1,0:T(2,128)S(1)}, f32[2,32]{1,0:T(2,128)S(1)}) all-reduce(f32[2,32]{1,0:T(2,128)S(1)} %get-tuple-element.6, f32[2,32]{1,0:T(2,128)S(1)} %get-tuple-element.5), channel_id=1, replica_groups=mesh['rep'=2,'gx'=16] {'gx'}, use_global_device_ids=true, to_apply=%region_3.0 | all-reduce | flops 128 | bytes 1024 | tf_op jit(solution)/shard_map/psum | solution.py:29
  43.3 1.7 fusion.37
  45.1 1.7 fusion.28
  46.8 0.6 dynamic-slice
  47.9 59.0 %all-reduce.3 = bf16[32,2,512]{2,0,1:T(8,128)(2,1)S(1)} all-reduce(f32[32,2,512]{2,0,1:T(8,128)S(1)} %fusion.28), channel_id=2, replica_groups=mesh['rep'=2,'gx'=16] {'gx'}, use_global_device_ids=true, to_apply=%region_5.6.clone | all-reduce | flops 32768 | bytes 196608
  106.9 0.1 iota_compare_fusion
  107.0 0.0 all-gather.3.cloned.1.call-done
  107.1 14.7 %fusion.25 = bf16[2,32,768]{2,1,0:T(8,128)(2,1)S(1)} fusion(bf16[2,32,18432]{2,1,0:T(8,128)(2,1)} %all-gather.3.cloned.1.call-done, bf16[18432,768]{1,0:T(8,128)(2,1)} %param.10), kind=kOutput, calls=%fused_computation.21 | convolution fusion | flops 1811988480 | bytes 30769152 | tf_op jit(solution)/shard_map/dot_general | solution.py:39
  121.8 0.7 copy.13
  122.5 3.5 %all-to-all-start = ((bf16[2,32,768]{2,0,1:T(2,128)(2,1)}), bf16[2,32,768]{2,0,1:T(2,128)(2,1)S(1)}, u32[]{:S(2)}, u32[]{:S(2)}) async-start(bf16[2,32,768]{2,0,1:T(2,128)(2,1)} %copy.13), calls=%async_computation | async-start | bytes 196608 | tf_op jit(solution)/shard_map/all_to_all | solution.py:90
  126.0 0.0 all-gather.5.cloned.1.call-start
  126.1 7.3 %all-to-all-done = bf16[2,32,768]{2,0,1:T(2,128)(2,1)S(1)} async-done(((bf16[2,32,768]{2,0,1:T(2,128)(2,1)}), bf16[2,32,768]{2,0,1:T(2,128)(2,1)S(1)}, u32[]{:S(2)}, u32[]{:S(2)}) %all-to-all-start) | async-done | bytes 98336 | tf_op jit(solution)/shard_map/all_to_all | solution.py:90
  133.4 0.1 reshape.60
  133.5 0.2 fusion.44
  133.7 0.8 fusion.43
  134.6 0.4 fusion.13
  135.0 0.2 convolution_bitcast_fusion
  135.2 0.1 copy-done.3
  135.3 0.5 fusion.22
  135.8 0.7 reshape.61
  136.5 37.2 %all-gather.5.cloned.1.call-done = bf16[2,32,12288]{2,0,1:T(2,128)(2,1)} async-done(((bf16[2,2,12288]{2,0,1:T(2,128)(2,1)}), bf16[2,32,12288]{2,0,1:T(2,128)(2,1)}) %all-gather.5.cloned.1.call-update) | async-done | bytes 1572880 | tf_op jit(solution)/shard_map/all_gather | solution.py:82
  173.7 15.8 %fusion.6 = bf16[2,32,1152]{2,1,0:T(8,128)(2,1)} fusion(bf16[12288,1152]{1,0:T(8,128)(2,1)} %param.12, bf16[2,32,12288]{2,0,1:T(2,128)(2,1)} %all-gather.5.cloned.1.call-done), kind=kOutput, calls=%fused_computation.7 | convolution fusion | flops 1812013056 | bytes 30031872 | tf_op jit(solution)/shard_map/dot_general | solution.py:84
  (20 shorter events, 0.2 us)
Async XLA Ops:
  6.5 127.1 %copy-start = (bf16[2,2048,256]{2,1,0:T(8,128)(2,1)S(1)}, bf16[2,2048,256]{2,1,0:T(8,128)(2,1)}, u32[]{:S(2)}) copy-start(bf16[2,2048,256]{2,1,0:T(8,128)(2,1)} %param.13) | copy-start | bytes 6291460
  6.5 40.2 %copy-start.4 = (u32[32]{0:T(128)S(1)}, u32[32]{0:T(128)}, u32[]{:S(2)}) copy-start(u32[32]{0:T(128)} %constant.18) | copy-start | bytes 388
  6.5 100.4 %copy-start.2 = (s32[2]{0:T(128)S(1)}, s32[2]{0:T(128)}, u32[]{:S(2)}) copy-start(s32[2]{0:T(128)} %param.15) | copy-start | bytes 28
  6.5 100.5 %all-gather.3.cloned.1.call-start = ((), (), s32[]{:S(2)}) async-start(), calls=%async_computation.1 | async-start | bytes 2506752 | tf_op jit(solution)/shard_map/all_gather | solution.py:37
  122.5 10.9 %all-to-all-start = ((bf16[2,32,768]{2,0,1:T(2,128)(2,1)}), bf16[2,32,768]{2,0,1:T(2,128)(2,1)S(1)}, u32[]{:S(2)}, u32[]{:S(2)}) async-start(bf16[2,32,768]{2,0,1:T(2,128)(2,1)} %copy.13), calls=%async_computation | async-start | bytes 196608 | tf_op jit(solution)/shard_map/all_to_all | solution.py:90
  126.0 47.7 %all-gather.5.cloned.1.call-start = ((), (), s32[]{:S(2)}) async-start(), calls=%async_computation.2 | async-start | bytes 1671168 | tf_op jit(solution)/shard_map/all_gather | solution.py:82
  133.7 1.6 copy-start.3
  173.7 15.8 %copy-start.1 = (bf16[2,2048,256]{2,1,0:T(8,128)(2,1)S(1)}, bf16[2,2048,256]{2,1,0:T(8,128)(2,1)}, u32[]{:S(2)}) copy-start(bf16[2,2048,256]{2,1,0:T(8,128)(2,1)} %param.13) | copy-start | bytes 6291460
Sparse Core Ops, SparseCore 0:
  45.2 39.6 all-gather.2
  136.6 37.0 all-gather.4

commit v2 on v1

--- a/solution.py
+++ b/solution.py
@@ -9,6 +9,7 @@
 D = 18432
 H = 48
 DH = 256
+CACHE = 2048
 
 
 EPS = 1e-05
@@ -94,6 +95,421 @@
     return finish(attended, w_out)
 
 
+GROUP = 16
+WIDTH = 1152
+PART_ROWS = 64
+QCOLS = 768
+MESH = pl.DeviceIdType.MESH
+
+
+def one_hots():
+    scatter_q = np.zeros((3, 256, 64), np.float32)
+    scatter_kv = np.zeros((128, 64), np.float32)
+    pack = np.zeros((192, 256), np.float32)
+    unpack = np.zeros((256, 256), np.float32)
+    for j in range(16):
+        for r in range(2):
+            for s in range(2):
+                row = s * 32 + 2 * j + r
+                scatter_kv[j * 8 + r * 2 + s, row] = 1
+                scatter_kv[j * 8 + 4 + r * 2 + s, row] = 1
+                for h in range(3):
+                    scatter_q[h, j * 16 + r * 8 + s * 3 + h, row] = 1
+                    pack[(j * 3 + h) * 4 + r * 2 + s, r * 128 + j * 8 + s * 3 + h] = 1
+                for h in range(4):
+                    unpack[h * 64 + row, j * 16 + h * 4 + r * 2 + s] = 1
+    return tuple(jnp.asarray(a, jnp.bfloat16) for a in (scatter_q, scatter_kv, pack, unpack))
+
+
+def dot(a, b):
+    return jnp.dot(a, b, preferred_element_type=jnp.float32)
+
+
+def dot_t(a, b):
+    return lax.dot_general(a, b, (((1,), (1,)), ((), ())), preferred_element_type=jnp.float32)
+
+
+def fused_kernel(
+    x_hbm, g_ref, wq_hbm, wkv_hbm, wo_hbm, kc_hbm, vc_hbm, len_ref, sq_hbm, skv_hbm, pack_hbm, unpack_hbm,
+    o_ref,
+    xg, w, wkv, kc, vc, sq, skv, pack, unpack, st_out, st_in, kv_out, kv_in, q_out, q_in, ag, xn, acc, oacc,
+    load_sem, wq_sem, wo_sem, x_send, x_recv, a_send, a_recv, st_send, st_recv, kv_send, kv_recv, q_send, q_recv,
+):
+    me = lax.axis_index("gx")
+    z = lax.div(me, 4)
+    y = lax.rem(lax.div(me, 2), 2)
+    c = lax.rem(me, 2)
+
+    def slot_of(zo, yo, co):
+        return zo * 4 + yo * 2 + co
+
+    def order(k):
+        near = jnp.minimum(z, 3 - z)
+        o = k if k >= 2 else jnp.where(near == 0, k, 1 - k)
+        return jnp.where(z >= 2, 3 - o, o)
+
+    own_load = pltpu.make_async_copy(x_hbm, xg.at[me], load_sem.at[0])
+    own_load.start()
+    wkv_load = pltpu.make_async_copy(wkv_hbm, wkv, load_sem.at[1])
+    wkv_load.start()
+    skv_load = pltpu.make_async_copy(skv_hbm, skv, load_sem.at[2])
+    skv_load.start()
+
+    def wq_load(chip):
+        rows = pl.ds(pl.multiple_of(chip * (2 * WIDTH), 2 * WIDTH), 2 * WIDTH)
+        return pltpu.make_async_copy(wq_hbm.at[rows], w.at[rows], wq_sem.at[chip])
+
+    chips = [(0, 0), (0, 1), (1, 0), (1, 1), (2, 0), (2, 1), (3, 0), (3, 1)]
+
+    def chip_of(k, flip):
+        return order(k) * 2 + (1 - y if flip else y)
+
+    for k, flip in chips:
+        wq_load(chip_of(k, flip)).start()
+    late_loads = [
+        pltpu.make_async_copy(sq_hbm, sq, load_sem.at[3]),
+        pltpu.make_async_copy(kc_hbm, kc, load_sem.at[4]),
+        pltpu.make_async_copy(vc_hbm, vc, load_sem.at[5]),
+        pltpu.make_async_copy(pack_hbm, pack, load_sem.at[6]),
+        pltpu.make_async_copy(unpack_hbm, unpack, load_sem.at[7]),
+    ]
+    for load in late_loads:
+        load.start()
+
+    barrier = pltpu.get_barrier_semaphore()
+    for step in range(1, GROUP):
+        pl.semaphore_signal(
+            barrier, inc=1, device_id={"gx": lax.rem(me + step, GROUP)}, device_id_type=MESH
+        )
+    pl.semaphore_wait(barrier, GROUP - 1)
+
+    def remote(src, dst, send, recv, dev):
+        return pltpu.make_async_remote_copy(
+            src_ref=src, dst_ref=dst, send_sem=send, recv_sem=recv, device_id={"gx": dev}, device_id_type=MESH
+        )
+
+    class Gather:
+        def __init__(self, buf, send, recv):
+            self.buf, self.send, self.recv = buf, send, recv
+
+        def copy(self, slot, k, kind, dev):
+            return remote(
+                self.buf.at[slot], self.buf.at[slot], self.send.at[k, kind], self.recv.at[slot], dev
+            )
+
+        def arrive(self, slot):
+            self.copy(slot, 0, 0, lax.rem(me + 1, GROUP)).wait_recv()
+
+        def line(self, k, act):
+            zo = order(k)
+            slot = slot_of(zo, y, c)
+
+            @pl.when(jnp.logical_and(zo <= z, z < 3))
+            def _():
+                act(self.copy(slot, k, 0, slot_of(z + 1, y, c)))
+
+            @pl.when(jnp.logical_and(zo >= z, z > 0))
+            def _():
+                act(self.copy(slot, k, 1, slot_of(z - 1, y, c)))
+
+            act(self.copy(slot, k, 2, slot_of(z, 1 - y, c)))
+            act(self.copy(slot, k, 3, slot_of(z, y, 1 - c)))
+
+        def across(self, k, act):
+            act(self.copy(slot_of(order(k), 1 - y, c), k, 4, slot_of(z, y, 1 - c)))
+
+        def step_line(self, k):
+            if k > 0:
+                self.arrive(slot_of(order(k), y, c))
+            self.line(k, lambda copy: copy.start())
+
+        def step_across(self, k):
+            self.arrive(slot_of(order(k), 1 - y, c))
+            self.across(k, lambda copy: copy.start())
+
+        def sibling(self, k, flip):
+            self.arrive(slot_of(order(k), 1 - y if flip else y, 1 - c))
+
+        def drain(self):
+            for k in range(4):
+                self.line(k, lambda copy: copy.wait_send())
+                self.across(k, lambda copy: copy.wait_send())
+
+    def spread(out, into, send, recv):
+        def copy(step):
+            target = lax.rem(me + step, GROUP)
+            return remote(out.at[target], into.at[me], send.at[step], recv.at[me], target)
+
+        for step in range(1, GROUP):
+            copy(step).start()
+        into[me] = out[me]
+        return copy
+
+    def collect(out, into, send, recv):
+        for step in range(1, GROUP):
+            source = lax.rem(me + step, GROUP)
+            remote(out.at[source], into.at[source], send.at[step], recv.at[source], source).wait_recv()
+
+    xs = Gather(xg, x_send, x_recv)
+    own_load.wait()
+    xs.step_line(0)
+
+    x = xg[me]
+    eye = lax.broadcasted_iota(jnp.int32, (PART_ROWS, PART_ROWS), 0) == lax.broadcasted_iota(
+        jnp.int32, (PART_ROWS, PART_ROWS), 1
+    )
+    squares = jnp.sum(jnp.where(eye, dot_t(x, x), 0.0), axis=0, keepdims=True)
+    sums = dot_t(jnp.ones((8, WIDTH), jnp.bfloat16), x)
+    st_out[...] = jnp.zeros_like(st_out)
+    st_out[0:9, :] = g_ref[...]
+    st_out[9:10, 0:PART_ROWS] = sums[0:1]
+    st_out[10:11, 0:PART_ROWS] = squares
+
+    def st_copy(step):
+        target = lax.rem(me + step, GROUP)
+        return remote(st_out, st_in.at[me], st_send.at[step], st_recv.at[me], target)
+
+    for step in range(1, GROUP):
+        st_copy(step).start()
+    st_in[me] = st_out[...]
+    for step in range(1, GROUP):
+        source = lax.rem(me + step, GROUP)
+        remote(st_out, st_in.at[source], st_send.at[step], st_recv.at[source], source).wait_recv()
+
+    total = st_in[0]
+    for source in range(1, GROUP):
+        total = total + st_in[source]
+
+    def column(row):
+        spread_row = jnp.broadcast_to(row, (PART_ROWS, PART_ROWS))
+        return jnp.sum(jnp.where(eye, spread_row, 0.0), axis=1, keepdims=True)
+
+    mean = column(total[9:10, 0:PART_ROWS]) / D
+    square = column(total[10:11, 0:PART_ROWS]) / D
+    factor = lax.rsqrt(square - mean * mean + EPS)
+
+    def normed(slot):
+        parts = st_in[slot]
+        gain = jnp.concatenate([parts[i : i + 1, :] for i in range(9)], axis=1)
+        return ((xg[slot].astype(jnp.float32) - mean) * factor * gain).astype(jnp.bfloat16)
+
+    wkv_load.wait()
+    skv_load.wait()
+    ordered = dot(skv[...], normed(me)).astype(jnp.bfloat16)
+    partial = dot(ordered, wkv[...])
+    is_key = lax.rem(lax.broadcasted_iota(jnp.int32, (128, DH), 0), 8) < 4
+    kv_out[...] = jnp.where(is_key, partial[:, :DH], partial[:, DH:]).reshape(GROUP, 8, DH)
+    kv_copy = spread(kv_out, kv_in, kv_send, kv_recv)
+
+    acc[...] = jnp.zeros_like(acc)
+
+    def multiply(k, flip):
+        chip = chip_of(k, flip)
+        xs.sibling(k, flip)
+        xn[:, 0:WIDTH] = normed(chip * 2)
+        xn[:, WIDTH : 2 * WIDTH] = normed(chip * 2 + 1)
+        wq_load(chip).wait()
+
+        def tile(i, carry):
+            rows = pl.ds(pl.multiple_of(chip * (2 * WIDTH) + i * 768, 768), 768)
+            acc[...] += dot(xn[:, pl.ds(pl.multiple_of(i * 768, 768), 768)], w[rows, :])
+            return carry
+
+        lax.fori_loop(0, 3, tile, 0)
+
+    xs.step_line(1)
+    xs.step_across(0)
+    multiply(0, 0)
+    xs.step_line(2)
+    xs.step_across(1)
+    multiply(0, 1)
+    multiply(1, 0)
+    xs.step_line(3)
+    xs.step_across(2)
+    multiply(1, 1)
+    multiply(2, 0)
+    xs.step_across(3)
+    multiply(2, 1)
+    multiply(3, 0)
+    multiply(3, 1)
+
+    half = H * DH // 2
+    rest = WIDTH - QCOLS
+    wo_loads = [
+        pltpu.make_async_copy(wo_hbm.at[:, pl.ds(0, QCOLS)], w.at[pl.ds(0, 2 * half)], wo_sem.at[0]),
+        pltpu.make_async_copy(
+            wo_hbm.at[pl.ds(0, half), pl.ds(QCOLS, rest)],
+            w.at[pl.ds(2 * half, half), pl.ds(0, rest)],
+            wo_sem.at[1],
+        ),
+        pltpu.make_async_copy(
+            wo_hbm.at[pl.ds(half, half), pl.ds(QCOLS, rest)],
+            w.at[pl.ds(2 * half, half), pl.ds(rest, rest)],
+            wo_sem.at[2],
+        ),
+    ]
+    for load in wo_loads:
+        load.start()
+    for load in late_loads:
+        load.wait()
+
+    queries = acc[...].astype(jnp.bfloat16)
+    placed = dot(sq[0], queries[:, 0:DH])
+    placed = placed + dot(sq[1], queries[:, DH : 2 * DH])
+    placed = placed + dot(sq[2], queries[:, 2 * DH : 3 * DH])
+    q_out[...] = placed.astype(jnp.bfloat16).reshape(GROUP, 16, DH)
+    q_copy = spread(q_out, q_in, q_send, q_recv)
+
+    collect(kv_out, kv_in, kv_send, kv_recv)
+    fresh = kv_in[0]
+    for source in range(1, GROUP):
+        fresh = fresh + kv_in[source]
+    fresh = fresh.astype(jnp.bfloat16).astype(jnp.float32)
+    blank = jnp.zeros((120, DH), jnp.float32)
+    fresh_keys = jnp.concatenate([fresh, blank], axis=0).astype(jnp.bfloat16)
+    fresh_values = jnp.concatenate([fresh[4:8], fresh[0:4], blank], axis=0).astype(jnp.bfloat16)
+
+    collect(q_out, q_in, q_send, q_recv)
+    wide = q_in[...].astype(jnp.float32)
+    scale = DH ** (-0.5)
+    column_at = lax.broadcasted_iota(jnp.int32, (128, CACHE), 1)
+    recent_at = lax.broadcasted_iota(jnp.int32, (128, 128), 1)
+    place = lax.rem(lax.broadcasted_iota(jnp.int32, (128, 128), 0), 8)
+    step_at = jnp.where(place >= 3, 1, 0)
+    results = []
+    for r in range(2):
+        q = wide[:, r * 8 : r * 8 + 8, :].reshape(128, DH).astype(jnp.bfloat16)
+        cached = jnp.where(column_at < len_ref[r], dot_t(q, kc[r]) * scale, -jnp.inf)
+        seen = jnp.logical_and(recent_at >= 2 * r, recent_at - 2 * r <= step_at)
+        recent = jnp.where(seen, dot_t(q, fresh_keys) * scale, -jnp.inf)
+        top = jnp.maximum(jnp.max(cached, -1, keepdims=True), jnp.max(recent, -1, keepdims=True))
+        cached_exp = jnp.exp(cached - top)
+        recent_exp = jnp.exp(recent - top)
+        denom = jnp.sum(cached_exp, -1, keepdims=True) + jnp.sum(recent_exp, -1, keepdims=True)
+        inverse = 1.0 / denom
+        result = dot((cached_exp * inverse).astype(jnp.bfloat16), vc[r])
+        result = result + dot((recent_exp * inverse).astype(jnp.bfloat16), fresh_values)
+        results.append(result.astype(jnp.bfloat16))
+    ag[me] = dot(pack[...], jnp.concatenate(results, axis=0)).astype(jnp.bfloat16)
+
+    gathered = Gather(ag, a_send, a_recv)
+    gathered.step_line(0)
+    gathered.step_line(1)
+    gathered.step_across(0)
+    gathered.step_line(2)
+    gathered.step_across(1)
+    gathered.step_line(3)
+    gathered.step_across(2)
+    gathered.step_across(3)
+    for k in range(4):
+        gathered.sibling(k, 0)
+        gathered.sibling(k, 1)
+    for load in wo_loads:
+        load.wait()
+
+    oacc[...] = jnp.zeros_like(oacc)
+    for upper in range(2):
+
+        def heads(i, carry):
+            g = i + upper * 6
+            block = ag[:, pl.ds(pl.multiple_of(g * 16, 16), 16), :].reshape(256, DH)
+            block = dot(unpack[...], block).astype(jnp.bfloat16)
+            left = oacc[:, 0:QCOLS]
+            right = oacc[:, QCOLS:WIDTH]
+            for h in range(4):
+                lhs = block[h * 64 : h * 64 + 64]
+                rows = pl.ds(pl.multiple_of((g * 4 + h) * DH, DH), DH)
+                left = left + dot(lhs, w[rows, :])
+                rows = pl.ds(pl.multiple_of(2 * half + (i * 4 + h) * DH, DH), DH)
+                right = right + dot(lhs, w[rows, upper * rest : upper * rest + rest])
+            oacc[:, 0:QCOLS] = left
+            oacc[:, QCOLS:WIDTH] = right
+            return carry
+
+        lax.fori_loop(0, 6, heads, 0)
+    o_ref[...] = oacc[...].astype(jnp.bfloat16)
+
+    for step in range(1, GROUP):
+        st_copy(step).wait_send()
+        kv_copy(step).wait_send()
+        q_copy(step).wait_send()
+    xs.drain()
+    gathered.drain()
+
+
+def fused(inputs, gain, w_query, w_keyval, w_out, key_cache, value_cache, lengths):
+    anywhere = pl.BlockSpec(memory_space=pl.ANY)
+    vmem = pl.BlockSpec(memory_space=pltpu.VMEM)
+    smem = pl.BlockSpec(memory_space=pltpu.SMEM)
+    bf16, f32 = jnp.bfloat16, jnp.float32
+    dma = pltpu.SemaphoreType.DMA
+    out = pl.pallas_call(
+        fused_kernel,
+        out_shape=jax.ShapeDtypeStruct((PART_ROWS, WIDTH), bf16),
+        in_specs=[anywhere, vmem] + [anywhere] * 5 + [smem] + [anywhere] * 4,
+        out_specs=vmem,
+        scratch_shapes=[
+            pltpu.VMEM((GROUP, PART_ROWS, WIDTH), bf16),
+            pltpu.VMEM((D, QCOLS), bf16),
+            pltpu.VMEM((WIDTH, 2 * DH), bf16),
+            pltpu.VMEM((2, CACHE, DH), bf16),
+            pltpu.VMEM((2, CACHE, DH), bf16),
+            pltpu.VMEM((3, 256, 64), bf16),
+            pltpu.VMEM((128, 64), bf16),
+            pltpu.VMEM((192, 256), bf16),
+            pltpu.VMEM((256, 256), bf16),
+            pltpu.VMEM((16, 128), f32),
+            pltpu.VMEM((GROUP, 16, 128), f32),
+            pltpu.VMEM((GROUP, 8, DH), f32),
+            pltpu.VMEM((GROUP, 8, DH), f32),
+            pltpu.VMEM((GROUP, 16, DH), bf16),
+            pltpu.VMEM((GROUP, 16, DH), bf16),
+            pltpu.VMEM((GROUP, 192, DH), bf16),
+            pltpu.VMEM((PART_ROWS, 2 * WIDTH), bf16),
+            pltpu.VMEM((PART_ROWS, QCOLS), f32),
+            pltpu.VMEM((PART_ROWS, WIDTH), f32),
+            dma((8,)),
+            dma((8,)),
+            dma((3,)),
+            dma((4, 5)),
+            dma((GROUP,)),
+            dma((4, 5)),
+            dma((GROUP,)),
+            dma((GROUP,)),
+            dma((GROUP,)),
+            dma((GROUP,)),
+            dma((GROUP,)),
+            dma((GROUP,)),
+            dma((GROUP,)),
+        ],
+        compiler_params=pltpu.CompilerParams(
+            collective_id=0, has_side_effects=True, vmem_limit_bytes=56 * 1024 * 1024
+        ),
+    )(
+        inputs.reshape(PART_ROWS, WIDTH),
+        gain.astype(f32).reshape(9, 128),
+        w_query,
+        w_keyval,
+        w_out,
+        key_cache,
+        value_cache,
+        lengths,
+        *one_hots(),
+    )
+    return out.reshape(inputs.shape)
+
+
+def either(inputs, gain, w_query, w_keyval, w_out, key_cache, value_cache, lengths):
+    fits = (
+        inputs.shape == (2, 32, WIDTH)
+        and w_query.shape == (D, QCOLS)
+        and w_out.shape == (H * DH, WIDTH)
+        and key_cache.shape == (2, CACHE, DH)
+    )
+    chosen = fused if fits else body
+    return chosen(inputs, gain, w_query, w_keyval, w_out, key_cache, value_cache, lengths)
+
+
 def solution(mesh):
     in_specs = (
         P(None, "rep", "gx"),
@@ -106,4 +522,4 @@
         P(("rep", "gx")),
     )
     out_specs = P(None, "rep", "gx")
-    return jax.shard_map(body, mesh=mesh, in_specs=in_specs, out_specs=out_specs, check_vma=False)
+    return jax.shard_map(either, mesh=mesh, in_specs=in_specs, out_specs=out_specs, check_vma=False)

time: 197 us -> 73.1 us (0.37)
  blocking collectives: 93.9 us -> 0 us
  Pallas kernels: 0 us -> 69.1 us
  waiting for transfers between devices: 44.5 us -> 0 us
  matrix products: 34 us -> 0 us
  between operations: 14.1 us -> 0.01 us
  starting transfers between devices: 3.55 us -> 0 us
  other arithmetic: 4.07 us -> 1.29 us
    pallas_call x0 -> x1, Pallas kernels: none -> 69.1 us  [fused(): pl.pallas_call(fused_kernel, out_shape=jax.ShapeDtypeStruct((PART_ROWS, W...]
    unnamed x1 -> x0, blocking collectives: 59 us -> none
    all_gather x2 -> x0, waiting for transfers between devices: 37.2 us -> none  [the longest x1 37.2 us: finish(): portion = lax.all_gather(attended, 'gx', axis=1, tiled=True)]
    psum x1 -> x0, blocking collectives: 34.9 us -> none  [project(): lax.psum((jnp.sum(widened, -1), jnp.sum(widened * widened, -1)), 'gx')]
    dot_general x7 -> x0, matrix products: 34 us -> none  [the longest x1 15.8 us: finish(): product = jnp.dot(flat, w_out, preferred_element_type=jnp.float32)]
    all_to_all x1 -> x0, waiting for transfers between devices: 7.27 us -> none  [body(): lax.all_to_all(queries, 'gx', split_axis=1, concat_axis=2, tiled=True)]
    all_to_all x1 -> x0, starting transfers between devices: 3.51 us -> none  [body(): lax.all_to_all(queries, 'gx', split_axis=1, concat_axis=2, tiled=True)]
    convert_element_type x2 -> x0, other arithmetic: 2.38 us -> none  [the longest x1 1.69 us: project(): normed = ((widened - row_mean) * lax.rsqrt(row_square - row_mean * row_me...]
  transfers between devices with their start and end apart: 3 -> 0, of which waited for: 2 -> 0; matrix products, arithmetic and copies ran while one was open for 1% -> 0% of each run, Pallas kernels for 0% -> 0%
where the time goes in v2:
time: 73.1 us; the launch traced here: 72 us
  Pallas kernels  69.1 us (95%)
  local copies, waits for them, and re-layouts  1.58 us (2%)
  other arithmetic  1.29 us (2%)
    pallas_call x1, Pallas kernels, fused(): pl.pallas_call(fused_kernel, out_shape=jax.ShapeDtypeStruct((PART_ROWS, W...  69.1 us
    unnamed x1, local copies, waits for them, and re-layouts  1.58 us

profile of v2, /device:TPU:0, one launch (start us, length us, event | category | flops | bytes accessed | tf_op | source)
XLA Modules:
  0.0 72.0 jit_solution(2999012490025168538)
XLA Ops:
  0.0 1.3 %bitcast_convert_fusion.g_ref = f32[9,128]{1,0:T(8,128)} fusion(bf16[1152]{0:T(1024)(128)(2,1)} %param.13), kind=kLoop, calls=%fused_computation | loop fusion | flops 1152 | bytes 6912 | tf_op jit(solution)/shard_map/reshape | solution.py:490
  1.3 69.1 %shard_map.118 = bf16[64,1152]{1,0:T(8,128)(2,1)} custom-call(bf16[64,1152]{1,0:T(8,128)(2,1)} %bitcast.6, f32[9,128]{1,0:T(8,128)} %bitcast_convert_fusion.g_ref, bf16[18432,768]{1,0:T(8,128)(2,1)} %wq_hbm.1, bf16[1152,512]{1,0:T(8,128)(2,1)} %wkv_hbm.1, bf16[12288,1152]{1,0:T(8,128)(2,1)} %wo_hbm.1, bf16[2,2048,256]{2,1,0:T(8,128)(2,1)} %kc_hbm.1, ...), custom_call_target="tpu_custom_call" | custom-call | tf_op jit(solution)/shard_map/pallas_call | solution.py:446
  70.4 1.6 %copy.14 = bf16[2,32,1152]{2,1,0:T(8,128)(2,1)} copy(bf16[2,32,1152]{2,1,0:T(8,128)(2,1)} %bitcast.5) | data formatting | bytes 294912

commit v3 on v2

--- a/solution.py
+++ b/solution.py
@@ -96,6 +96,8 @@
 
 
 GROUP = 16
+UNROLL = 6
+PIECES = 2
 WIDTH = 1152
 PART_ROWS = 64
 QCOLS = 768
@@ -132,7 +134,7 @@
 def fused_kernel(
     x_hbm, g_ref, wq_hbm, wkv_hbm, wo_hbm, kc_hbm, vc_hbm, len_ref, sq_hbm, skv_hbm, pack_hbm, unpack_hbm,
     o_ref,
-    xg, w, wkv, kc, vc, sq, skv, pack, unpack, st_out, st_in, kv_out, kv_in, q_out, q_in, ag, xn, acc, oacc,
+    xg, w, wkv, kc, vc, sq, skv, pack, unpack, st_out, st_in, kv_out, kv_in, q_out, q_in, ag, lhs_of, xn, acc, oacc,
     load_sem, wq_sem, wo_sem, x_send, x_recv, a_send, a_recv, st_send, st_recv, kv_send, kv_recv, q_send, q_recv,
 ):
     me = lax.axis_index("gx")
@@ -189,51 +191,60 @@
         )
 
     class Gather:
-        def __init__(self, buf, send, recv):
-            self.buf, self.send, self.recv = buf, send, recv
-
-        def copy(self, slot, k, kind, dev):
-            return remote(
-                self.buf.at[slot], self.buf.at[slot], self.send.at[k, kind], self.recv.at[slot], dev
-            )
-
-        def arrive(self, slot):
-            self.copy(slot, 0, 0, lax.rem(me + 1, GROUP)).wait_recv()
-
-        def line(self, k, act):
+        def __init__(self, buf, send, recv, pieces):
+            self.buf, self.send, self.recv, self.pieces = buf, send, recv, pieces
+            self.rows = buf.shape[1] // pieces
+
+        def copy(self, slot, k, p, kind, dev):
+            block = self.buf.at[slot, pl.ds(p * self.rows, self.rows)]
+            return remote(block, block, self.send.at[k, p, kind], self.recv.at[slot, p], dev)
+
+        def arrive(self, slot, p):
+            self.copy(slot, 0, p, 0, lax.rem(me + 1, GROUP)).wait_recv()
+
+        def own_across(self):
+            return self.copy(me, 0, 0, 2, slot_of(z, 1 - y, c))
+
+        def line(self, k, p, act, skip=False):
             zo = order(k)
             slot = slot_of(zo, y, c)
 
             @pl.when(jnp.logical_and(zo <= z, z < 3))
             def _():
-                act(self.copy(slot, k, 0, slot_of(z + 1, y, c)))
+                act(self.copy(slot, k, p, 0, slot_of(z + 1, y, c)))
 
             @pl.when(jnp.logical_and(zo >= z, z > 0))
             def _():
-                act(self.copy(slot, k, 1, slot_of(z - 1, y, c)))
-
-            act(self.copy(slot, k, 2, slot_of(z, 1 - y, c)))
-            act(self.copy(slot, k, 3, slot_of(z, y, 1 - c)))
-
-        def across(self, k, act):
-            act(self.copy(slot_of(order(k), 1 - y, c), k, 4, slot_of(z, y, 1 - c)))
-
-        def step_line(self, k):
-            if k > 0:
-                self.arrive(slot_of(order(k), y, c))
-            self.line(k, lambda copy: copy.start())
-
-        def step_across(self, k):
-            self.arrive(slot_of(order(k), 1 - y, c))
-            self.across(k, lambda copy: copy.start())
-
-        def sibling(self, k, flip):
-            self.arrive(slot_of(order(k), 1 - y if flip else y, 1 - c))
+                act(self.copy(slot, k, p, 1, slot_of(z - 1, y, c)))
+
+            if not skip:
+                act(self.copy(slot, k, p, 2, slot_of(z, 1 - y, c)))
+            act(self.copy(slot, k, p, 3, slot_of(z, y, 1 - c)))
+
+        def across(self, k, p, act):
+            act(self.copy(slot_of(order(k), 1 - y, c), k, p, 4, slot_of(z, y, 1 - c)))
+
+        def step(self, k):
+            for p in range(self.pieces):
+                if k < 4:
+                    if k > 0:
+                        self.arrive(slot_of(order(k), y, c), p)
+                    self.line(k, p, lambda copy: copy.start())
+                if k == 0 and p == 0:
+                    self.own_across().wait_send()
+                if k > 0:
+                    self.arrive(slot_of(order(k - 1), 1 - y, c), p)
+                    self.across(k - 1, p, lambda copy: copy.start())
+
+        def sibling(self, k, flip, pieces=range(PIECES)):
+            for p in pieces:
+                self.arrive(slot_of(order(k), 1 - y if flip else y, 1 - c), p)
 
         def drain(self):
             for k in range(4):
-                self.line(k, lambda copy: copy.wait_send())
-                self.across(k, lambda copy: copy.wait_send())
+                for p in range(self.pieces):
+                    self.line(k, p, lambda copy: copy.wait_send(), k == 0 and p == 0)
+                    self.across(k, p, lambda copy: copy.wait_send())
 
     def spread(out, into, send, recv):
         def copy(step):
@@ -250,9 +261,9 @@
             source = lax.rem(me + step, GROUP)
             remote(out.at[source], into.at[source], send.at[step], recv.at[source], source).wait_recv()
 
-    xs = Gather(xg, x_send, x_recv)
+    xs = Gather(xg, x_send, x_recv, PIECES)
     own_load.wait()
-    xs.step_line(0)
+    xs.step(0)
 
     x = xg[me]
     eye = lax.broadcasted_iota(jnp.int32, (PART_ROWS, PART_ROWS), 0) == lax.broadcasted_iota(
@@ -261,7 +272,7 @@
     squares = jnp.sum(jnp.where(eye, dot_t(x, x), 0.0), axis=0, keepdims=True)
     sums = dot_t(jnp.ones((8, WIDTH), jnp.bfloat16), x)
     st_out[...] = jnp.zeros_like(st_out)
-    st_out[0:9, :] = g_ref[...]
+    st_out[0:9, :] = g_ref[...].astype(jnp.float32).reshape(9, 128)
     st_out[9:10, 0:PART_ROWS] = sums[0:1]
     st_out[10:11, 0:PART_ROWS] = squares
 
@@ -272,6 +283,7 @@
     for step in range(1, GROUP):
         st_copy(step).start()
     st_in[me] = st_out[...]
+    xs.step(1)
     for step in range(1, GROUP):
         source = lax.rem(me + step, GROUP)
         remote(st_out, st_in.at[source], st_send.at[step], st_recv.at[source], source).wait_recv()
@@ -310,27 +322,19 @@
         xn[:, WIDTH : 2 * WIDTH] = normed(chip * 2 + 1)
         wq_load(chip).wait()
 
-        def tile(i, carry):
-            rows = pl.ds(pl.multiple_of(chip * (2 * WIDTH) + i * 768, 768), 768)
-            acc[...] += dot(xn[:, pl.ds(pl.multiple_of(i * 768, 768), 768)], w[rows, :])
-            return carry
-
-        lax.fori_loop(0, 3, tile, 0)
-
-    xs.step_line(1)
-    xs.step_across(0)
+        rows = pl.ds(pl.multiple_of(chip * (2 * WIDTH), 2 * WIDTH), 2 * WIDTH)
+        acc[...] += dot(xn[...], w[rows, :])
+
+    xs.step(2)
     multiply(0, 0)
-    xs.step_line(2)
-    xs.step_across(1)
     multiply(0, 1)
     multiply(1, 0)
-    xs.step_line(3)
-    xs.step_across(2)
+    xs.step(3)
     multiply(1, 1)
     multiply(2, 0)
-    xs.step_across(3)
     multiply(2, 1)
     multiply(3, 0)
+    xs.step(4)
     multiply(3, 1)
 
     half = H * DH // 2
@@ -392,41 +396,40 @@
         results.append(result.astype(jnp.bfloat16))
     ag[me] = dot(pack[...], jnp.concatenate(results, axis=0)).astype(jnp.bfloat16)
 
-    gathered = Gather(ag, a_send, a_recv)
-    gathered.step_line(0)
-    gathered.step_line(1)
-    gathered.step_across(0)
-    gathered.step_line(2)
-    gathered.step_across(1)
-    gathered.step_line(3)
-    gathered.step_across(2)
-    gathered.step_across(3)
-    for k in range(4):
-        gathered.sibling(k, 0)
-        gathered.sibling(k, 1)
+    gathered = Gather(ag, a_send, a_recv, PIECES)
+    for k in range(5):
+        gathered.step(k)
     for load in wo_loads:
         load.wait()
 
     oacc[...] = jnp.zeros_like(oacc)
-    for upper in range(2):
+    for upper in range(PIECES):
+        for k in range(4):
+            gathered.sibling(k, 0, (upper,))
+            gathered.sibling(k, 1, (upper,))
 
         def heads(i, carry):
-            g = i + upper * 6
-            block = ag[:, pl.ds(pl.multiple_of(g * 16, 16), 16), :].reshape(256, DH)
-            block = dot(unpack[...], block).astype(jnp.bfloat16)
+            for n in range(UNROLL):
+                t = i * UNROLL + n
+                g = t + upper * 6
+                block = ag[:, pl.ds(pl.multiple_of(g * 16, 16), 16), :].reshape(256, DH)
+                lhs_of[n] = dot(unpack[...], block).astype(jnp.bfloat16)
             left = oacc[:, 0:QCOLS]
             right = oacc[:, QCOLS:WIDTH]
-            for h in range(4):
-                lhs = block[h * 64 : h * 64 + 64]
-                rows = pl.ds(pl.multiple_of((g * 4 + h) * DH, DH), DH)
-                left = left + dot(lhs, w[rows, :])
-                rows = pl.ds(pl.multiple_of(2 * half + (i * 4 + h) * DH, DH), DH)
-                right = right + dot(lhs, w[rows, upper * rest : upper * rest + rest])
+            for n in range(UNROLL):
+                t = i * UNROLL + n
+                g = t + upper * 6
+                for h in range(4):
+                    lhs = lhs_of[n, h * 64 : h * 64 + 64]
+                    rows = pl.ds(pl.multiple_of((g * 4 + h) * DH, DH), DH)
+                    left = left + dot(lhs, w[rows, :])
+                    rows = pl.ds(pl.multiple_of(2 * half + (t * 4 + h) * DH, DH), DH)
+                    right = right + dot(lhs, w[rows, upper * rest : upper * rest + rest])
             oacc[:, 0:QCOLS] = left
             oacc[:, QCOLS:WIDTH] = right
             return carry
 
-        lax.fori_loop(0, 6, heads, 0)
+        lax.fori_loop(0, 6 // UNROLL, heads, 0)
     o_ref[...] = oacc[...].astype(jnp.bfloat16)
 
     for step in range(1, GROUP):
@@ -465,16 +468,17 @@
             pltpu.VMEM((GROUP, 16, DH), bf16),
             pltpu.VMEM((GROUP, 16, DH), bf16),
             pltpu.VMEM((GROUP, 192, DH), bf16),
+            pltpu.VMEM((UNROLL, 256, DH), bf16),
             pltpu.VMEM((PART_ROWS, 2 * WIDTH), bf16),
             pltpu.VMEM((PART_ROWS, QCOLS), f32),
             pltpu.VMEM((PART_ROWS, WIDTH), f32),
             dma((8,)),
             dma((8,)),
             dma((3,)),
-            dma((4, 5)),
-            dma((GROUP,)),
-            dma((4, 5)),
-            dma((GROUP,)),
+            dma((4, PIECES, 5)),
+            dma((GROUP, PIECES)),
+            dma((4, PIECES, 5)),
+            dma((GROUP, PIECES)),
             dma((GROUP,)),
             dma((GROUP,)),
             dma((GROUP,)),
@@ -487,7 +491,7 @@
         ),
     )(
         inputs.reshape(PART_ROWS, WIDTH),
-        gain.astype(f32).reshape(9, 128),
+        gain,
         w_query,
         w_keyval,
         w_out,

time: 73.1 us -> 66 us (0.903); the launches traced: 72 us -> 65.8 us
  Pallas kernels: 69.1 us -> 64.2 us
  other arithmetic: 1.29 us -> 0 us
    pallas_call x1, Pallas kernels: 69.1 us -> 64.2 us  [fused(): pl.pallas_call(fused_kernel, out_shape=jax.ShapeDtypeStruct((PART_ROWS, W...]
    reshape x1 -> x0, other arithmetic: 1.29 us -> none  [fused(): gain.astype(f32).reshape(9, 128)]
where the time goes in v3:
time: 66 us; the launch traced here: 65.8 us
  Pallas kernels  64.2 us (97%)
  local copies, waits for them, and re-layouts  1.58 us (2%)
    pallas_call x1, Pallas kernels, fused(): pl.pallas_call(fused_kernel, out_shape=jax.ShapeDtypeStruct((PART_ROWS, W...  64.2 us
    unnamed x1, local copies, waits for them, and re-layouts  1.58 us

profile of v3, /device:TPU:0, one launch (start us, length us, event | category | flops | bytes accessed | tf_op | source)
XLA Modules:
  0.0 65.8 jit_solution(18263290281329487489)
XLA Ops:
  0.0 64.2 %shard_map.118 = bf16[64,1152]{1,0:T(8,128)(2,1)} custom-call(bf16[64,1152]{1,0:T(8,128)(2,1)} %bitcast.3, bf16[1152]{0:T(1024)(128)(2,1)} %g_ref.1, bf16[18432,768]{1,0:T(8,128)(2,1)} %wq_hbm.1, bf16[1152,512]{1,0:T(8,128)(2,1)} %wkv_hbm.1, bf16[12288,1152]{1,0:T(8,128)(2,1)} %wo_hbm.1, bf16[2,2048,256]{2,1,0:T(8,128)(2,1)} %kc_hbm.1, ...), custom_call_target="tpu_custom_call" | custom-call | tf_op jit(solution)/shard_map/pallas_call | solution.py:449
  64.2 1.6 %copy.14 = bf16[2,32,1152]{2,1,0:T(8,128)(2,1)} copy(bf16[2,32,1152]{2,1,0:T(8,128)(2,1)} %bitcast.2) | data formatting | bytes 294912
